TPU v7x, 32 devices: a whole 2x2x4 slice. The times are simulated.
32 devices in a mesh: row: 4 (over y, x), col: 8 (over z, core).
Axes of the slice: x: 2, y: 2, z: 4, core: 2. Of those that a mesh axis runs over, the one named last changes fastest.
Arguments:
- sources: bfloat16 [8192, 1024], P(('row', 'col')), may hold values from -6 to 6
- leaf_in: bfloat16 [32, 256, 256], P(('row', 'col')), may hold values from -0.375 to 0.375
- transfers: bfloat16 [32, 5, 2, 256, 256], P(('row', 'col')), may hold values from -0.25 to 0.25
- leaf_out: bfloat16 [32, 256, 256], P(('row', 'col')), may hold values from -0.375 to 0.375
- tile_mats: bfloat16 [32, 5, 256, 256], P(('row', 'col')), may hold values from -0.375 to 0.375
- tile_list: int32 [32, 5], P(('row', 'col')), may hold values from 0 to 1, as said below
Outputs:
- applied: bfloat16 [8192, 1024], P(('row', 'col'))
Inputs may be any that keep to these rules, and one draw needn't show every extreme that they name: tile_list[b, k] is 1 where source block b holds a tile onto the block k - 2 places further along its row of 8 blocks; always 1 for k = 2, always 0 where that block lies outside the row; blocks hold different numbers of tiles.
All inputs are finite; a program needn't handle non-finite values.
Results may differ from a plain program's by a relative error of at most 0.015.
Values may be sent and summed in bfloat16 or wider, within the bound.
A program may use at most 64 MiB of HBM per device.

v0:
```python
import jax
import jax.numpy as jnp
from jax import lax
from jax.sharding import PartitionSpec as P

TILES = 5


def from_partner(block, axis, apart):
    count = lax.axis_size(axis)
    route = []
    for low in range(count):
        high = low | 1 << apart
        if high != low and high < count:
            route += [(low, high), (high, low)]
    return lax.ppermute(block, axis, route)


def from_behind(shard, axis, by):
    devices = lax.axis_size(axis)
    pairs = [(i, i + by) for i in range(devices) if 0 <= i + by < devices]
    return lax.ppermute(shard, axis, pairs)


def mixing(mats, vectors):
    return jnp.dot(mats, vectors, preferred_element_type=jnp.float32)


def shards(sources, leaf_in, transfers, leaf_out, tile_mats, tile_list):
    coeffs = mixing(leaf_in[0], sources).astype(jnp.bfloat16)
    levels_high = lax.axis_size("row").bit_length() - 1
    levels_low = lax.axis_size("col").bit_length() - 1
    for bit in range(levels_high):
        partner = from_partner(coeffs, "row", bit)
        coeffs = (
            mixing(transfers[0, bit, 0], coeffs) + mixing(transfers[0, bit, 1], partner)
        ).astype(jnp.bfloat16)
    for bit in range(levels_low):
        level = levels_high + bit
        partner = from_partner(coeffs, "col", bit)
        coeffs = (
            mixing(transfers[0, level, 0], coeffs) + mixing(transfers[0, level, 1], partner)
        ).astype(jnp.bfloat16)
    far = mixing(leaf_out[0], coeffs)
    live = tile_list[0].astype(jnp.float32)
    middle = TILES // 2
    near = live[middle] * mixing(tile_mats[0, middle], sources)
    for k in range(TILES):
        if k == middle:
            continue
        product = live[k] * mixing(tile_mats[0, k], sources)
        near = near + from_behind(product.astype(jnp.bfloat16), "col", k - middle).astype(
            product.dtype
        )
    return (far + near).astype(jnp.bfloat16)


def solution(mesh):
    return jax.shard_map(
        shards,
        mesh=mesh,
        in_specs=(
            P(("row", "col"), None),
            P(("row", "col"), None, None),
            P(("row", "col"), None, None, None, None),
            P(("row", "col"), None, None),
            P(("row", "col"), None, None, None),
            P(("row", "col"), None),
        ),
        out_specs=P(("row", "col"), None),
        check_vma=False,
    )
```

profile of v0, /device:TPU:1, one launch (start us, length us, event | category | flops | bytes accessed | tf_op | source)
XLA Modules:
  0.0 87.3 jit_solution(11403890169526125236)
XLA Ops:
  0.0 0.0 copy-start
  0.0 0.0 copy-start.1
  0.0 1.0 %copy-done = bf16[256,1024]{1,0:T(8,128)(2,1)S(1)} copy-done((bf16[256,1024]{1,0:T(8,128)(2,1)S(1)}, bf16[256,1024]{1,0:T(8,128)(2,1)}, u32[]{:S(2)}) %copy-start) | copy-done | bytes 524312
  1.0 1.2 %convolution_convert_fusion = bf16[256,1024]{1,0:T(8,128)(2,1)S(1)} fusion(bf16[256,1024]{1,0:T(8,128)(2,1)S(1)} %copy-done, bf16[1,256,256]{2,1,0:T(8,128)(2,1)} %param.7), kind=kOutput, calls=%fused_computation.11 | convolution fusion | flops 134479872 | bytes 1179648 | tf_op jit(solution)/shard_map/dot_general | solution.py:26
  2.3 2.1 %collective-permute-start = (bf16[256,1024]{1,0:T(8,128)(2,1)S(1)}, bf16[256,1024]{1,0:T(8,128)(2,1)S(1)}, u32[]{:S(2)}, u32[]{:S(2)}) collective-permute-start(bf16[256,1024]{1,0:T(8,128)(2,1)S(1)} %convolution_convert_fusion), channel_id=1, source_target_pairs={{0,8},{8,0},{16,24},{24,16},{1,9},{9,1},{17,25},{25,17},{2,10},{10... | collective-permute-start | bytes 1572872 | tf_op jit(solution)/shard_map/ppermute | solution.py:16
  4.4 1.3 %fusion.31 = f32[1024,256]{1,0:T(8,128)S(1)} fusion(bf16[256,1024]{1,0:T(8,128)(2,1)S(1)} %convolution_convert_fusion, bf16[1,5,2,256,256]{4,3,2,1,0:T(8,128)(2,1)} %param.8), kind=kOutput, calls=%fused_computation.42 | convolution fusion | flops 134217728 | bytes 1703936 | tf_op jit(solution)/shard_map/dot_general | solution.py:26
  5.6 0.0 copy-start.5
  5.6 10.4 %collective-permute-done = bf16[256,1024]{1,0:T(8,128)(2,1)S(1)} collective-permute-done((bf16[256,1024]{1,0:T(8,128)(2,1)S(1)}, bf16[256,1024]{1,0:T(8,128)(2,1)S(1)}, u32[]{:S(2)}, u32[]{:S(2)}) %collective-permute-start) | collective-permute-done | bytes 524320 | tf_op jit(solution)/shard_map/ppermute | solution.py:16
  16.0 0.0 copy-done.1
  16.0 0.4 fusion
  16.4 1.2 %collective-permute-start.1 = (bf16[256,1024]{0,1:T(8,128)(2,1)S(1)}, bf16[256,1024]{0,1:T(8,128)(2,1)S(1)}, u32[]{:S(2)}, u32[]{:S(2)}) collective-permute-start(bf16[256,1024]{0,1:T(8,128)(2,1)S(1)} %bitcast.86), channel_id=1, source_target_pairs={{0,16},{16,0},{8,24},{24,8},{1,17},{17,1},{9,25},{25,9},{2,18},{18... | collective-permute-start | bytes 1572872 | tf_op jit(solution)/shard_map/ppermute | solution.py:16
  17.6 0.0 copy-done.5
  17.6 0.7 fusion.50
  18.3 0.3 fusion.28
  18.6 0.0 copy-start.2
  18.6 10.0 %collective-permute-done.1 = bf16[256,1024]{0,1:T(8,128)(2,1)S(1)} collective-permute-done((bf16[256,1024]{0,1:T(8,128)(2,1)S(1)}, bf16[256,1024]{0,1:T(8,128)(2,1)S(1)}, u32[]{:S(2)}, u32[]{:S(2)}) %collective-permute-start.1) | collective-permute-done | bytes 524320 | tf_op jit(solution)/shard_map/ppermute | solution.py:16
  28.6 0.3 fusion.1
  29.0 2.2 %collective-permute-start.2 = (bf16[256,1024]{0,1:T(8,128)(2,1)S(1)}, bf16[256,1024]{0,1:T(8,128)(2,1)S(1)}, u32[]{:S(2)}, u32[]{:S(2)}) collective-permute-start(bf16[256,1024]{0,1:T(8,128)(2,1)S(1)} %bitcast.84), channel_id=1, source_target_pairs={{0,1},{1,0},{2,3},{3,2},{4,5},{5,4},{6,7},{7,6},{8,9},{9,8},{10,11... | collective-permute-start | bytes 1572872 | tf_op jit(solution)/shard_map/ppermute | solution.py:16
  31.2 0.0 copy-done.2
  31.2 0.9 %fusion.6 = bf16[256,1024]{0,1:T(8,128)(2,1)S(1)} fusion(bf16[256,1024]{1,0:T(8,128)(2,1)S(1)} %copy-done, f32[]{:T(128)} %bitcast.21, bf16[1,5,256,256]{3,2,1,0:T(8,128)(2,1)S(1)} %copy-done.2), kind=kOutput, calls=%fused_computation.18 | convolution fusion | flops 134742016 | bytes 1179652 | tf_op jit(solution)/shard_map/dot_general | solution.py:26
  32.1 1.9 %collective-permute-start.6 = (bf16[256,1024]{0,1:T(8,128)(2,1)S(1)}, bf16[256,1024]{0,1:T(8,128)(2,1)}, u32[]{:S(2)}, u32[]{:S(2)}) collective-permute-start(bf16[256,1024]{0,1:T(8,128)(2,1)S(1)} %fusion.6), channel_id=1, source_target_pairs={{1,0},{2,1},{3,2},{4,3},{5,4},{6,5},{7,6},{9,8},{10,9},{11,10},{12... | collective-permute-start | bytes 1572872 | tf_op jit(solution)/shard_map/ppermute | solution.py:22
  34.0 1.0 %fusion.7 = bf16[256,1024]{0,1:T(8,128)(2,1)S(1)} fusion(bf16[256,1024]{1,0:T(8,128)(2,1)S(1)} %copy-done, f32[]{:T(128)} %bitcast.23, bf16[1,5,256,256]{3,2,1,0:T(8,128)(2,1)S(1)} %copy-done.2), kind=kOutput, calls=%fused_computation.19 | convolution fusion | flops 134742016 | bytes 1179652 | tf_op jit(solution)/shard_map/dot_general | solution.py:26
  35.0 3.6 %collective-permute-start.7 = (bf16[256,1024]{0,1:T(8,128)(2,1)S(1)}, bf16[256,1024]{0,1:T(8,128)(2,1)}, u32[]{:S(2)}, u32[]{:S(2)}) collective-permute-start(bf16[256,1024]{0,1:T(8,128)(2,1)S(1)} %fusion.7), channel_id=1, source_target_pairs={{0,1},{1,2},{2,3},{3,4},{4,5},{5,6},{6,7},{8,9},{9,10},{10,11},{11... | collective-permute-start | bytes 1572872 | tf_op jit(solution)/shard_map/ppermute | solution.py:22
  38.6 0.3 fusion.25
  39.0 0.0 collective-permute-done.2
  39.0 0.3 fusion.2
  39.3 1.3 %collective-permute-start.3 = (bf16[256,1024]{0,1:T(8,128)(2,1)S(1)}, bf16[256,1024]{0,1:T(8,128)(2,1)S(1)}, u32[]{:S(2)}, u32[]{:S(2)}) collective-permute-start(bf16[256,1024]{0,1:T(8,128)(2,1)S(1)} %bitcast.85), channel_id=1, source_target_pairs={{0,2},{2,0},{1,3},{3,1},{4,6},{6,4},{5,7},{7,5},{8,10},{10,8},{9,1... | collective-permute-start | bytes 1572872 | tf_op jit(solution)/shard_map/ppermute | solution.py:16
  40.6 1.0 %fusion.8 = bf16[256,1024]{0,1:T(8,128)(2,1)S(1)} fusion(bf16[256,1024]{1,0:T(8,128)(2,1)S(1)} %copy-done, f32[]{:T(128)} %bitcast.25, bf16[1,5,256,256]{3,2,1,0:T(8,128)(2,1)S(1)} %copy-done.2), kind=kOutput, calls=%fused_computation.20 | convolution fusion | flops 134742016 | bytes 1179652 | tf_op jit(solution)/shard_map/dot_general | solution.py:26
  41.6 3.0 %collective-permute-start.8 = (bf16[256,1024]{0,1:T(8,128)(2,1)S(1)}, bf16[256,1024]{0,1:T(8,128)(2,1)}, u32[]{:S(2)}, u32[]{:S(2)}) collective-permute-start(bf16[256,1024]{0,1:T(8,128)(2,1)S(1)} %fusion.8), channel_id=1, source_target_pairs={{0,2},{1,3},{2,4},{3,5},{4,6},{5,7},{8,10},{9,11},{10,12},{11,13},... | collective-permute-start | bytes 1572872 | tf_op jit(solution)/shard_map/ppermute | solution.py:22
  44.6 1.0 %fusion.5 = bf16[256,1024]{0,1:T(8,128)(2,1)S(1)} fusion(bf16[256,1024]{1,0:T(8,128)(2,1)S(1)} %copy-done, f32[]{:T(128)} %bitcast.19, bf16[1,5,256,256]{3,2,1,0:T(8,128)(2,1)S(1)} %copy-done.2), kind=kOutput, calls=%fused_computation.17 | convolution fusion | flops 134742016 | bytes 1179652 | tf_op jit(solution)/shard_map/dot_general | solution.py:26
  45.6 1.3 %collective-permute-start.5 = (bf16[256,1024]{0,1:T(8,128)(2,1)S(1)}, bf16[256,1024]{0,1:T(8,128)(2,1)S(1)}, u32[]{:S(2)}, u32[]{:S(2)}) collective-permute-start(bf16[256,1024]{0,1:T(8,128)(2,1)S(1)} %fusion.5), channel_id=1, source_target_pairs={{2,0},{3,1},{4,2},{5,3},{6,4},{7,5},{10,8},{11,9},{12,10},{13,11},... | collective-permute-start | bytes 1572872 | tf_op jit(solution)/shard_map/ppermute | solution.py:22
  46.9 0.3 fusion.22
  47.2 13.0 %collective-permute-done.3 = bf16[256,1024]{0,1:T(8,128)(2,1)S(1)} collective-permute-done((bf16[256,1024]{0,1:T(8,128)(2,1)S(1)}, bf16[256,1024]{0,1:T(8,128)(2,1)S(1)}, u32[]{:S(2)}, u32[]{:S(2)}) %collective-permute-start.3) | collective-permute-done | bytes 524320 | tf_op jit(solution)/shard_map/ppermute | solution.py:16
  60.2 0.3 fusion.3
  60.5 7.1 %collective-permute-start.4 = (bf16[256,1024]{0,1:T(8,128)(2,1)S(1)}, bf16[256,1024]{0,1:T(8,128)(2,1)}, u32[]{:S(2)}, u32[]{:S(2)}) collective-permute-start(bf16[256,1024]{0,1:T(8,128)(2,1)S(1)} %bitcast.83), channel_id=1, source_target_pairs={{0,4},{4,0},{1,5},{5,1},{2,6},{6,2},{3,7},{7,3},{8,12},{12,8},{9,1... | collective-permute-start | bytes 1572872 | tf_op jit(solution)/shard_map/ppermute | solution.py:16
  67.7 0.0 copy-start.4
  67.7 0.9 %convolution_multiply_fusion.4 = f32[256,1024]{0,1:T(8,128)S(1)} fusion(bf16[256,1024]{1,0:T(8,128)(2,1)S(1)} %copy-done, f32[]{:T(128)} %bitcast.17, bf16[1,5,256,256]{3,2,1,0:T(8,128)(2,1)S(1)} %copy-done.2), kind=kOutput, calls=%fused_computation.4 | convolution fusion | flops 134479872 | bytes 1703940 | tf_op jit(solution)/shard_map/dot_general | solution.py:26
  68.6 0.3 fusion.19
  69.0 0.0 collective-permute-done.6
  69.0 0.0 collective-permute-done.7
  69.0 2.5 %collective-permute-done.8 = bf16[256,1024]{0,1:T(8,128)(2,1)} collective-permute-done((bf16[256,1024]{0,1:T(8,128)(2,1)S(1)}, bf16[256,1024]{0,1:T(8,128)(2,1)}, u32[]{:S(2)}, u32[]{:S(2)}) %collective-permute-start.8) | collective-permute-done | bytes 524320 | tf_op jit(solution)/shard_map/ppermute | solution.py:22
  71.4 0.0 collective-permute-done.5
  71.4 0.0 copy-start.3
  71.4 0.8 copy-done.3
  72.2 11.7 %collective-permute-done.4 = bf16[256,1024]{0,1:T(8,128)(2,1)} collective-permute-done((bf16[256,1024]{0,1:T(8,128)(2,1)S(1)}, bf16[256,1024]{0,1:T(8,128)(2,1)}, u32[]{:S(2)}, u32[]{:S(2)}) %collective-permute-start.4) | collective-permute-done | bytes 524320 | tf_op jit(solution)/shard_map/ppermute | solution.py:16
  84.0 0.0 copy-done.4
  84.0 2.3 %fusion.10 = bf16[256,1024]{0,1:T(8,128)(2,1)S(1)} fusion(f32[1024,256]{1,0:T(8,128)S(1)} %fusion.19, bf16[256,1024]{0,1:T(8,128)(2,1)} %collective-permute-done.4, bf16[256,1024]{0,1:T(8,128)(2,1)} %collective-permute-done.8, bf16[256,1024]{0,1:T(8,128)(2,1)} %collective-permute-done.7, bf16[256,1024]{0,1:T(8,128)(2,1)} %collective-permute-done.6, ...), kind=kOutput, calls=%fused_computation.22 | convolution fusion | flops 271581184 | bytes 5505024 | tf_op jit(solution)/shard_map/dot_general | solution.py:26
  86.3 1.0 %copy.12 = bf16[256,1024]{1,0:T(8,128)(2,1)} copy(bf16[256,1024]{0,1:T(8,128)(2,1)S(1)} %fusion.10) | data formatting | bytes 1048576 | tf_op jit(solution)/shard_map/convert_element_type | solution.py:55
  (1 shorter events, 0.0 us)
Async XLA Ops:
  0.0 1.0 %copy-start = (bf16[256,1024]{1,0:T(8,128)(2,1)S(1)}, bf16[256,1024]{1,0:T(8,128)(2,1)}, u32[]{:S(2)}) copy-start(bf16[256,1024]{1,0:T(8,128)(2,1)} %param.6) | copy-start | bytes 1572868
  0.0 16.0 %copy-start.1 = (bf16[1,5,2,256,256]{4,3,2,1,0:T(8,128)(2,1)S(1)}, bf16[1,5,2,256,256]{4,3,2,1,0:T(8,128)(2,1)}, u32[]{:S(2)}) copy-start(bf16[1,5,2,256,256]{4,3,2,1,0:T(8,128)(2,1)} %param.8) | copy-start | bytes 3932164
  2.3 13.8 %collective-permute-start = (bf16[256,1024]{1,0:T(8,128)(2,1)S(1)}, bf16[256,1024]{1,0:T(8,128)(2,1)S(1)}, u32[]{:S(2)}, u32[]{:S(2)}) collective-permute-start(bf16[256,1024]{1,0:T(8,128)(2,1)S(1)} %convolution_convert_fusion), channel_id=1, source_target_pairs={{0,8},{8,0},{16,24},{24,16},{1,9},{9,1},{17,25},{25,17},{2,10},{10... | collective-permute-start | bytes 1572872 | tf_op jit(solution)/shard_map/ppermute | solution.py:16
  5.6 12.0 %copy-start.5 = (s32[1,5]{1,0:T(1,128)S(1)}, s32[1,5]{1,0:T(1,128)}, u32[]{:S(2)}) copy-start(s32[1,5]{1,0:T(1,128)} %param.11) | copy-start | bytes 64
  16.4 12.3 %collective-permute-start.1 = (bf16[256,1024]{0,1:T(8,128)(2,1)S(1)}, bf16[256,1024]{0,1:T(8,128)(2,1)S(1)}, u32[]{:S(2)}, u32[]{:S(2)}) collective-permute-start(bf16[256,1024]{0,1:T(8,128)(2,1)S(1)} %bitcast.86), channel_id=1, source_target_pairs={{0,16},{16,0},{8,24},{24,8},{1,17},{17,1},{9,25},{25,9},{2,18},{18... | collective-permute-start | bytes 1572872 | tf_op jit(solution)/shard_map/ppermute | solution.py:16
  18.6 12.6 %copy-start.2 = (bf16[1,5,256,256]{3,2,1,0:T(8,128)(2,1)S(1)}, bf16[1,5,256,256]{3,2,1,0:T(8,128)(2,1)}, u32[]{:S(2)}) copy-start(bf16[1,5,256,256]{3,2,1,0:T(8,128)(2,1)} %param.10) | copy-start | bytes 1966084
  29.0 10.0 %collective-permute-start.2 = (bf16[256,1024]{0,1:T(8,128)(2,1)S(1)}, bf16[256,1024]{0,1:T(8,128)(2,1)S(1)}, u32[]{:S(2)}, u32[]{:S(2)}) collective-permute-start(bf16[256,1024]{0,1:T(8,128)(2,1)S(1)} %bitcast.84), channel_id=1, source_target_pairs={{0,1},{1,0},{2,3},{3,2},{4,5},{5,4},{6,7},{7,6},{8,9},{9,8},{10,11... | collective-permute-start | bytes 1572872 | tf_op jit(solution)/shard_map/ppermute | solution.py:16
  32.1 36.9 %collective-permute-start.6 = (bf16[256,1024]{0,1:T(8,128)(2,1)S(1)}, bf16[256,1024]{0,1:T(8,128)(2,1)}, u32[]{:S(2)}, u32[]{:S(2)}) collective-permute-start(bf16[256,1024]{0,1:T(8,128)(2,1)S(1)} %fusion.6), channel_id=1, source_target_pairs={{1,0},{2,1},{3,2},{4,3},{5,4},{6,5},{7,6},{9,8},{10,9},{11,10},{12... | collective-permute-start | bytes 1572872 | tf_op jit(solution)/shard_map/ppermute | solution.py:22
  35.0 34.0 %collective-permute-start.7 = (bf16[256,1024]{0,1:T(8,128)(2,1)S(1)}, bf16[256,1024]{0,1:T(8,128)(2,1)}, u32[]{:S(2)}, u32[]{:S(2)}) collective-permute-start(bf16[256,1024]{0,1:T(8,128)(2,1)S(1)} %fusion.7), channel_id=1, source_target_pairs={{0,1},{1,2},{2,3},{3,4},{4,5},{5,6},{6,7},{8,9},{9,10},{10,11},{11... | collective-permute-start | bytes 1572872 | tf_op jit(solution)/shard_map/ppermute | solution.py:22
  39.3 20.9 %collective-permute-start.3 = (bf16[256,1024]{0,1:T(8,128)(2,1)S(1)}, bf16[256,1024]{0,1:T(8,128)(2,1)S(1)}, u32[]{:S(2)}, u32[]{:S(2)}) collective-permute-start(bf16[256,1024]{0,1:T(8,128)(2,1)S(1)} %bitcast.85), channel_id=1, source_target_pairs={{0,2},{2,0},{1,3},{3,1},{4,6},{6,4},{5,7},{7,5},{8,10},{10,8},{9,1... | collective-permute-start | bytes 1572872 | tf_op jit(solution)/shard_map/ppermute | solution.py:16
  41.6 29.8 %collective-permute-start.8 = (bf16[256,1024]{0,1:T(8,128)(2,1)S(1)}, bf16[256,1024]{0,1:T(8,128)(2,1)}, u32[]{:S(2)}, u32[]{:S(2)}) collective-permute-start(bf16[256,1024]{0,1:T(8,128)(2,1)S(1)} %fusion.8), channel_id=1, source_target_pairs={{0,2},{1,3},{2,4},{3,5},{4,6},{5,7},{8,10},{9,11},{10,12},{11,13},... | collective-permute-start | bytes 1572872 | tf_op jit(solution)/shard_map/ppermute | solution.py:22
  45.6 25.9 %collective-permute-start.5 = (bf16[256,1024]{0,1:T(8,128)(2,1)S(1)}, bf16[256,1024]{0,1:T(8,128)(2,1)S(1)}, u32[]{:S(2)}, u32[]{:S(2)}) collective-permute-start(bf16[256,1024]{0,1:T(8,128)(2,1)S(1)} %fusion.5), channel_id=1, source_target_pairs={{2,0},{3,1},{4,2},{5,3},{6,4},{7,5},{10,8},{11,9},{12,10},{13,11},... | collective-permute-start | bytes 1572872 | tf_op jit(solution)/shard_map/ppermute | solution.py:22
  60.5 23.4 %collective-permute-start.4 = (bf16[256,1024]{0,1:T(8,128)(2,1)S(1)}, bf16[256,1024]{0,1:T(8,128)(2,1)}, u32[]{:S(2)}, u32[]{:S(2)}) collective-permute-start(bf16[256,1024]{0,1:T(8,128)(2,1)S(1)} %bitcast.83), channel_id=1, source_target_pairs={{0,4},{4,0},{1,5},{5,1},{2,6},{6,2},{3,7},{7,3},{8,12},{12,8},{9,1... | collective-permute-start | bytes 1572872 | tf_op jit(solution)/shard_map/ppermute | solution.py:16
  67.7 16.3 %copy-start.4 = (bf16[1,256,256]{2,1,0:T(8,128)(2,1)S(1)}, bf16[1,256,256]{2,1,0:T(8,128)(2,1)}, u32[]{:S(2)}) copy-start(bf16[1,256,256]{2,1,0:T(8,128)(2,1)} %param.9) | copy-start | bytes 393220
  71.4 0.8 copy-start.3
where the time goes:
time: 87.6 us; the launch traced here: 87.3 us
  waiting for transfers between devices  47.6 us (54%)
  starting transfers between devices  23.8 us (27%)
  matrix products  12.2 us (14%)
  local copies, waits for them, and re-layouts  3.51 us (4%)
    ppermute x5, waiting for transfers between devices, from_partner(): return lax.ppermute(block, axis, route)  45.1 us
    ppermute x5, starting transfers between devices, from_partner(): return lax.ppermute(block, axis, route)  14 us
    dot_general x16, matrix products, mixing(): return jnp.dot(mats, vectors, preferred_element_type=jnp.float32)  12.2 us
    ppermute x4, starting transfers between devices, from_behind(): return lax.ppermute(shard, axis, pairs)  9.83 us
    ppermute x4, waiting for transfers between devices, from_behind(): return lax.ppermute(shard, axis, pairs)  2.47 us
    unnamed x12, local copies, waits for them, and re-layouts  1.85 us
  transfers between devices with their start and end apart: 9, of which 5 were waited for; matrix products, arithmetic and copies ran while one was open for 10% of the time, Pallas kernels for 0%

commit v1 on v0

v1 whole, which is shorter than its diff:
```python
import functools

import jax
import jax.numpy as jnp
from jax import lax
from jax.experimental import pallas as pl
from jax.experimental.pallas import tpu as pltpu
from jax.sharding import PartitionSpec as P

MESH = pl.DeviceIdType.MESH
CHUNKS = 4
VMEM_BYTES = 60 * 1024 * 1024


def dot(mats, vectors):
    return jnp.dot(mats, vectors, preferred_element_type=jnp.float32)


def level_plan(rows, cols):
    high = [("row", 1 << b) for b in range(rows.bit_length() - 1)]
    low = [("col", 1 << b) for b in range(cols.bit_length() - 1)]
    return high + low


def task_order(plan, chunks):
    when = {}
    for l, (axis, apart) in enumerate(plan):
        hop = 1.0 if axis == "row" else (0.25 if apart == 1 else 0.65 * apart)
        for c in range(chunks):
            ready = when[l - 1, c] if l else 0.1 * c
            free = when[l, c - 1] if c else 0.0
            when[l, c] = max(ready, free) + hop
    return sorted(when, key=lambda task: (when[task], task))


def kernel(plan, chunks, src, w_in, trans, w_out, tiles, live, out,
           s_own, s_peer, coef, got, win_v, tr_v, wout_v, tl_v, tm_v, tp_own, tp_peer,
           near_out, near_in, acc, out_v,
           src_sem, load_sem, lsend, lrecv, ssend, srecv, tsend, trecv, nsend, nrecv, osem):
    row, col = lax.axis_index("row"), lax.axis_index("col")
    cols = lax.axis_size("col")
    levels = len(plan)
    width = s_own.shape[-1]

    def load(source, target, sem):
        copy = pltpu.make_async_copy(source, target, sem)
        copy.start()
        return copy

    src_loads = []
    for c in range(chunks):
        src_loads.append(
            load(src.at[:, pl.ds(c * width, width)], s_own.at[c], src_sem.at[c])
        )
        if c == 0:
            win_load = load(w_in.at[0], win_v, load_sem.at[0])
            tile_load = load(tiles.at[0], tl_v, load_sem.at[1])
    trans_load = load(trans.at[0], tr_v, load_sem.at[2])
    wout_load = load(w_out.at[0], wout_v, load_sem.at[3])

    def partner(level):
        axis, apart = plan[level]
        at = row if axis == "row" else col
        other = at + apart * (1 - 2 * ((at // apart) % 2))
        return (other, col) if axis == "row" else (row, other)

    odd = col % 2
    step = 2 - 4 * odd
    peer = (row, col + 1 - 2 * odd)
    ahead, behind = col + step, col - step
    has_ahead = jnp.logical_and(ahead >= 0, ahead < cols)
    has_behind = jnp.logical_and(behind >= 0, behind < cols)

    barrier = pltpu.get_barrier_semaphore()
    for level in range(levels):
        pl.semaphore_signal(barrier, inc=1, device_id=partner(level), device_id_type=MESH)

    @pl.when(has_ahead)
    def _():
        pl.semaphore_signal(barrier, inc=1, device_id=(row, ahead), device_id_type=MESH)

    @pl.when(has_behind)
    def _():
        pl.semaphore_signal(barrier, inc=1, device_id=(row, behind), device_id_type=MESH)

    pl.semaphore_wait(
        barrier, levels + has_ahead.astype(jnp.int32) + has_behind.astype(jnp.int32)
    )

    @pl.when(jnp.logical_not(has_behind))
    def _():
        near_in[0] = jnp.zeros_like(near_in[0])

    @pl.when(jnp.logical_not(has_ahead))
    def _():
        near_in[1] = jnp.zeros_like(near_in[1])

    def level_copy(level, c):
        return pltpu.make_async_remote_copy(
            src_ref=coef.at[level, c], dst_ref=got.at[level, c],
            send_sem=lsend.at[level, c], recv_sem=lrecv.at[level, c],
            device_id=partner(level), device_id_type=MESH)

    def source_copy(c):
        return pltpu.make_async_remote_copy(
            src_ref=s_own.at[c], dst_ref=s_peer.at[c],
            send_sem=ssend.at[c], recv_sem=srecv.at[c],
            device_id=peer, device_id_type=MESH)

    tile_copy = pltpu.make_async_remote_copy(
        src_ref=tp_own, dst_ref=tp_peer, send_sem=tsend.at[0], recv_sem=trecv.at[0],
        device_id=peer, device_id_type=MESH)

    def near_copy(way, c):
        to = ahead if way == 0 else behind
        return pltpu.make_async_remote_copy(
            src_ref=near_out.at[way, c], dst_ref=near_in.at[way, c],
            send_sem=nsend.at[way, c], recv_sem=nrecv.at[way, c],
            device_id=(row, to), device_id_type=MESH)

    for c in range(chunks):
        src_loads[c].wait()
        source_copy(c).start()
        if c == 0:
            win_load.wait()
        coef[0, c] = dot(win_v[...], s_own[c]).astype(coef.dtype)
        level_copy(0, c).start()
        if c == 0:
            tile_load.wait()
            for k in range(tl_v.shape[0]):
                kept = tl_v[k].astype(jnp.float32) * live[0, k].astype(jnp.float32)
                kept = kept.astype(tm_v.dtype)
                tm_v[k] = kept
                if k in (1, 3):
                    tp_own[k // 2] = kept
            tile_copy.start()

        @pl.when(has_behind)
        def _():
            near_out[1, c] = dot(tm_v[4 * odd], s_own[c]).astype(near_out.dtype)
            near_copy(1, c).start()

    tile_copy.wait_recv()
    for c in range(chunks):
        source_copy(c).wait_recv()

        @pl.when(has_ahead)
        def _():
            total = dot(tm_v[4 - 4 * odd], s_own[c]) + dot(tp_peer[1 - odd], s_peer[c])
            near_out[0, c] = total.astype(near_out.dtype)
            near_copy(0, c).start()

    for c in range(chunks):
        acc[c] = dot(tm_v[2], s_own[c]) + dot(tp_peer[odd], s_peer[c])

    trans_load.wait()
    wout_load.wait()
    stores = []
    for level, c in task_order(plan, chunks):
        last = level == levels - 1
        if last:
            @pl.when(has_behind)
            def _():
                near_copy(0, c).wait_recv()

            @pl.when(has_ahead)
            def _():
                near_copy(1, c).wait_recv()

            acc[c] += near_in[0, c].astype(jnp.float32) + near_in[1, c].astype(jnp.float32)

        level_copy(level, c).wait_recv()
        mixed = dot(tr_v[level, 0], coef[level, c]) + dot(tr_v[level, 1], got[level, c])
        mixed = mixed.astype(coef.dtype)
        if last:
            out_v[c] = (dot(wout_v[...], mixed) + acc[c]).astype(out_v.dtype)
            stores.append(
                load(out_v.at[c], out.at[:, pl.ds(c * width, width)], osem.at[c])
            )
        else:
            coef[level + 1, c] = mixed
            level_copy(level + 1, c).start()

    tile_copy.wait_send()
    for c in range(chunks):
        source_copy(c).wait_send()
        for level in range(levels):
            level_copy(level, c).wait_send()

        @pl.when(has_ahead)
        def _():
            near_copy(0, c).wait_send()

        @pl.when(has_behind)
        def _():
            near_copy(1, c).wait_send()

    for store in stores:
        store.wait()


def shards(sources, leaf_in, transfers, leaf_out, tile_mats, tile_list):
    plan = level_plan(lax.axis_size("row"), lax.axis_size("col"))
    levels = len(plan)
    rank, vecs = sources.shape
    count = tile_mats.shape[1]
    chunks = CHUNKS
    width = vecs // chunks
    half = jnp.bfloat16
    block = (chunks, rank, width)
    dma = pltpu.SemaphoreType.DMA
    anywhere = pl.BlockSpec(memory_space=pl.ANY)
    flops = 2 * rank * rank * vecs * (2 * levels + count + 4)
    return pl.pallas_call(
        functools.partial(kernel, plan, chunks),
        out_shape=jax.ShapeDtypeStruct((rank, vecs), half),
        in_specs=[anywhere] * 5 + [pl.BlockSpec(memory_space=pltpu.SMEM)],
        out_specs=anywhere,
        scratch_shapes=[
            pltpu.VMEM(block, half),
            pltpu.VMEM(block, half),
            pltpu.VMEM((levels,) + block, half),
            pltpu.VMEM((levels,) + block, half),
            pltpu.VMEM((rank, rank), half),
            pltpu.VMEM((levels, 2, rank, rank), half),
            pltpu.VMEM((rank, rank), half),
            pltpu.VMEM((count, rank, rank), half),
            pltpu.VMEM((count, rank, rank), half),
            pltpu.VMEM((2, rank, rank), half),
            pltpu.VMEM((2, rank, rank), half),
            pltpu.VMEM((2,) + block, half),
            pltpu.VMEM((2,) + block, half),
            pltpu.VMEM(block, jnp.float32),
            pltpu.VMEM(block, half),
            dma((chunks,)),
            dma((4,)),
            dma((levels, chunks)),
            dma((levels, chunks)),
            dma((chunks,)),
            dma((chunks,)),
            dma((1,)),
            dma((1,)),
            dma((2, chunks)),
            dma((2, chunks)),
            dma((chunks,)),
        ],
        compiler_params=pltpu.CompilerParams(
            collective_id=0, has_side_effects=True, vmem_limit_bytes=VMEM_BYTES
        ),
        cost_estimate=pl.CostEstimate(
            flops=flops, bytes_accessed=8 * 1024 * 1024, transcendentals=0
        ),
    )(sources, leaf_in, transfers, leaf_out, tile_mats, tile_list)


def solution(mesh):
    return jax.shard_map(
        shards,
        mesh=mesh,
        in_specs=(
            P(("row", "col"), None),
            P(("row", "col"), None, None),
            P(("row", "col"), None, None, None, None),
            P(("row", "col"), None, None),
            P(("row", "col"), None, None, None),
            P(("row", "col"), None),
        ),
        out_specs=P(("row", "col"), None),
        check_vma=False,
    )
```

time: 87.6 us -> 51.4 us (0.59)
  Pallas kernels: 0 us -> 48.7 us
  waiting for transfers between devices: 47.6 us -> 0 us
  starting transfers between devices: 23.8 us -> 0 us
  matrix products: 12.2 us -> 0 us
  local copies, waits for them, and re-layouts: 3.51 us -> 1.87 us
    pallas_call x0 -> x1, Pallas kernels: none -> 48.7 us  [shards(): pl.pallas_call(functools.partial(kernel, plan, chunks), out_shape=jax.Sha...]
    ppermute x9 -> x0, waiting for transfers between devices: 47.6 us -> none  [the longest x5 45.1 us: from_partner(): return lax.ppermute(block, axis, route)]
    ppermute x9 -> x0, starting transfers between devices: 23.8 us -> none  [the longest x5 14 us: from_partner(): return lax.ppermute(block, axis, route)]
    dot_general x16 -> x0, matrix products: 12.2 us -> none  [mixing(): return jnp.dot(mats, vectors, preferred_element_type=jnp.float32)]
    convert_element_type x1 -> x0, local copies, waits for them, and re-layouts: 1 us -> none  [shards(): return (far + near).astype(jnp.bfloat16)]
    unnamed x12 -> x1, local copies, waits for them, and re-layouts: 1.85 us -> 1.87 us
  transfers between devices with their start and end apart: 9 -> 0, of which waited for: 5 -> 0; matrix products, arithmetic and copies ran while one was open for 10% -> 0% of each run, Pallas kernels for 0% -> 0%
where the time goes in v1:
time: 51.4 us; the launch traced here: 50.5 us
  Pallas kernels  48.7 us (95%)
  local copies, waits for them, and re-layouts  1.87 us (4%)
    pallas_call x1, Pallas kernels, shards(): pl.pallas_call(functools.partial(kernel, plan, chunks), out_shape=jax.Sha...  48.7 us
    unnamed x1, local copies, waits for them, and re-layouts  1.87 us

profile of v1, /device:TPU:1, one launch (start us, length us, event | category | flops | bytes accessed | tf_op | source)
XLA Modules:
  0.0 50.5 jit_solution(17658784549176283529)
XLA Ops:
  0.0 48.7 %shard_map.64 = bf16[256,1024]{1,0:T(8,128)(2,1)} custom-call(bf16[256,1024]{1,0:T(8,128)(2,1)} %src.1, bf16[1,256,256]{2,1,0:T(8,128)(2,1)} %w_in.1, bf16[1,5,2,256,256]{4,3,2,1,0:T(8,128)(2,1)} %trans.1, bf16[1,256,256]{2,1,0:T(8,128)(2,1)} %w_out.1, bf16[1,5,256,256]{3,2,1,0:T(8,128)(2,1)} %tiles.1, s32[1,5]{1,0:T(1,128)} %live.1), custom_call_target="tpu_custom_call" | custom-call | flops 2550136832 | bytes 8388608 | tf_op jit(solution)/shard_map/pallas_call | solution.py:214
  48.7 1.9 %copy.8 = bf16[256,1024]{1,0:T(8,128)(2,1)} copy(bf16[256,1024]{1,0:T(8,128)(2,1)} %shard_map.64) | data formatting | bytes 1048576
